TPU v7x, 256 devices: a whole 4x4x8 slice. The times are simulated.
256 devices in a mesh: dp: 16 (over z, core), expert: 16 (over x, y).
Axes of the slice: x: 4, y: 4, z: 8, core: 2. Of those that a mesh axis runs over, the one named last changes fastest.
Arguments:
- activations: bfloat16 [16384, 8, 768], P(('dp', 'expert')), may hold values from -6 to 6
- out_grad: bfloat16 [16384, 2048], P(('dp', 'expert')), may hold values from -0.796875 to 0.796875
- gate_weights: float32 [16384, 8], P(('dp', 'expert')), may hold values from 0.02 to 0.3
- routes: int32 [16384, 8], P(('dp', 'expert')), may hold values from 0 to 63, all different within a row; in each aligned block of 64 rows (0 to 63, 64 to 127, ...) at most 16 rows name the same one
- momentum: float32 [131072, 768], P(('expert', 'dp')), may hold values from -4 to 4
Outputs:
- update: bfloat16 [131072, 768], P(('expert', 'dp'))
- new_momentum: float32 [131072, 768], P(('expert', 'dp'))
Inputs may be any that keep to these rules, and one draw needn't show every extreme that they name: `routes`: each row names 8 different experts. Among the 64 rows of one device no expert is named by more than 16 rows, and in every draw some expert is named by exactly 16 rows of some device.
All inputs are finite; a program needn't handle non-finite values.
Results may differ from a plain program's by a relative error of at most 0.029.
Values may be sent and summed in bfloat16 or wider, within the bound.
A program may use at most 128 MiB of HBM per device.

v0:
```python
import math
import jax
import jax.numpy as jnp
from jax import lax
from jax.sharding import PartitionSpec as P

EXP_DEV = 4
NS_ITERS = 2
MOMENT = 0.95
COEFF_A = 3.4445
COEFF_B = -4.775
COEFF_C = 2.0315
EPSILON = 1e-07


def swapped(block, axis, apart):
    count = lax.axis_size(axis)
    route = []
    for low in range(count):
        high = low | 1 << apart
        if high != low and high < count:
            route += [(low, high), (high, low)]
    return lax.ppermute(block, axis, route)


def slot_table(routing, expert_total, capacity):
    tokens_here = routing.shape[0]
    slots_token = routing.shape[1]
    numbers = jnp.arange(expert_total, dtype=jnp.int32)
    matched = (routing[:, :, None] == numbers[None, None, :]).astype(jnp.int32)
    named_by = jnp.sum(matched, axis=1)
    position = jnp.sum(matched * jnp.arange(slots_token, dtype=jnp.int32)[None, :, None], axis=1)
    earlier = jnp.cumsum(named_by, axis=0) - named_by
    places = jnp.arange(capacity, dtype=jnp.int32)
    picked = ((named_by[:, :, None] == 1) & (earlier[:, :, None] == places[None, None, :])).astype(
        jnp.int32
    )
    pair_index = jnp.arange(tokens_here, dtype=jnp.int32)[:, None] * slots_token + position
    source = jnp.sum(picked * pair_index[:, :, None], axis=0)
    filled = jnp.sum(picked, axis=0) > 0
    return (source, filled)


def pack_slots(hidden_block, grad_block, gate_block, source, filled, slots_token):
    hidden_rows = hidden_block.reshape(-1, hidden_block.shape[-1])
    picked_rows = jnp.where(
        filled[..., None], jnp.take(hidden_rows, source, axis=0), jnp.zeros((), hidden_rows.dtype)
    )
    scales = jnp.where(filled, jnp.take(gate_block.reshape(-1), source), jnp.zeros((), jnp.float32))
    grad_rows = jnp.take(grad_block, source // slots_token, axis=0).astype(jnp.float32)
    weighted = (scales[..., None] * grad_rows).astype(jnp.bfloat16)
    return (picked_rows, weighted)


def newton_update(scaled, gram):
    square = jnp.dot(gram, gram, preferred_element_type=jnp.float32)
    poly = (COEFF_B * gram.astype(jnp.float32) + COEFF_C * square).astype(jnp.bfloat16)
    product = jnp.dot(scaled, poly, preferred_element_type=jnp.float32)
    return (COEFF_A * scaled.astype(jnp.float32) + product).astype(jnp.bfloat16)


def gram_of(scaled):
    return lax.dot_general(
        scaled, scaled, (((0,), (0,)), ((), ())), preferred_element_type=jnp.float32
    )


def body(activations, out_grad, gate_weights, routes, momentum):
    expert_count = lax.axis_size("expert")
    dp_count = lax.axis_size("dp")
    tokens_here = routes.shape[0]
    slots_token = routes.shape[1]
    expert_total = EXP_DEV * expert_count
    capacity = min(tokens_here, 2 * tokens_here * slots_token // expert_total)
    model_width = out_grad.shape[1]
    hidden_width = activations.shape[2]
    own_rows = momentum.shape[0]
    group_size = dp_count // EXP_DEV
    levels = group_size.bit_length() - 1
    source, filled = slot_table(routes, expert_total, capacity)
    source = (
        source.reshape(expert_count, EXP_DEV, capacity)
        .transpose(1, 0, 2)
        .reshape(EXP_DEV, expert_count * capacity)
    )
    filled = (
        filled.reshape(expert_count, EXP_DEV, capacity)
        .transpose(1, 0, 2)
        .reshape(EXP_DEV, expert_count * capacity)
    )
    hidden_send, weighted_send = pack_slots(
        activations, out_grad, gate_weights, source, filled, slots_token
    )
    hidden_got, weighted_got = (
        lax.all_to_all(hidden_send, "expert", split_axis=1, concat_axis=1, tiled=True),
        lax.all_to_all(weighted_send, "expert", split_axis=1, concat_axis=1, tiled=True),
    )

    def block_rows(block_index):
        begin_row = block_index * own_rows
        expert_local = begin_row // model_width
        column = begin_row % model_width
        hidden_expert = lax.dynamic_index_in_dim(hidden_got, expert_local, 0, keepdims=False)
        weighted_expert = lax.dynamic_index_in_dim(weighted_got, expert_local, 0, keepdims=False)
        columns = lax.dynamic_slice_in_dim(weighted_expert, column, own_rows, 1)
        return lax.dot_general(
            columns, hidden_expert, (((0,), (0,)), ((), ())), preferred_element_type=jnp.float32
        )

    blocks = lax.map(
        block_rows, jnp.arange(own_rows * lax.axis_size("dp") // own_rows, dtype=jnp.int32)
    )
    gradient = lax.psum_scatter(
        blocks.reshape(own_rows * lax.axis_size("dp"), hidden_width).astype(jnp.bfloat16),
        "dp",
        scatter_dimension=0,
        tiled=True,
    ).astype(jnp.float32)
    new_momentum = MOMENT * momentum + gradient
    ahead = gradient + MOMENT * new_momentum
    rank_dp = lax.axis_index("dp")
    part_index = rank_dp % group_size
    gathered = ahead
    for bit_index in range(levels):
        other = swapped(gathered.astype(jnp.bfloat16), "dp", bit_index).astype(gathered.dtype)
        upper = rank_dp // 2**bit_index % 2
        gathered = jnp.where(
            upper == 0, jnp.concatenate([gathered, other], 0), jnp.concatenate([other, gathered], 0)
        )
    norm_value = jnp.sqrt(jnp.sum(gathered * gathered))
    scaled_whole = (gathered / (norm_value + EPSILON)).astype(jnp.bfloat16)
    for turn_index in range(NS_ITERS):
        gram = gram_of(scaled_whole).astype(jnp.bfloat16)
        scaled_whole = newton_update(scaled_whole, gram)
    scaled = lax.dynamic_slice_in_dim(scaled_whole, part_index * own_rows, own_rows, 0)
    update = (math.sqrt(model_width) * scaled.astype(jnp.float32)).astype(jnp.bfloat16)
    return (update, new_momentum)


def solution(mesh):
    in_specs = (
        P(("dp", "expert"), None, None),
        P(("dp", "expert"), None),
        P(("dp", "expert"), None),
        P(("dp", "expert"), None),
        P(("expert", "dp"), None),
    )
    out_specs = (P(("expert", "dp"), None), P(("expert", "dp"), None))
    return jax.shard_map(body, mesh=mesh, in_specs=in_specs, out_specs=out_specs, check_vma=False)
```

profile of v0, /device:TPU:1, one launch (start us, length us, event | category | flops | bytes accessed | tf_op | source)
XLA Modules:
  0.0 348.5 jit_solution(1447675559522099637)
XLA Ops:
  7.2 0.8 copy.28
  8.0 0.2 convert_reduce_fusion.1
  9.1 0.8 copy.33
  10.0 6.9 %gather_fusion = f32[1024]{0:T(1024)S(1)} fusion(f32[512]{0:T(512)S(1)} %reshape.202, s32[1024]{0:T(1024)S(1)} %broadcast_clamp_fusion.1), kind=kCustom, calls=%fused_computation | custom fusion | bytes 12288 | tf_op jit(solution)/shard_map/jit(_take)/gather | solution.py:49
  16.9 4.0 %gather_fusion.2 = bf16[1024,768]{1,0:T(8,128)(2,1)S(1)} fusion(bf16[512,768]{1,0:T(8,128)(2,1)S(1)} %bitcast.45, s32[1024]{0:T(1024)S(1)} %broadcast_clamp_fusion.1), kind=kCustom, calls=%fused_computation.2 | custom fusion | bytes 3149824 | tf_op jit(solution)/shard_map/jit(_take)/gather | solution.py:47
  21.3 4.3 %fusion.6 = bf16[4,256,768]{2,0,1:T(4,128)(2,1)} fusion(bf16[4,256,768]{2,1,0:T(8,128)(2,1)S(1)} %bitcast.48, pred[4,256]{0,1:T(8,128)(4,1)S(1)} %copy.39, pred[4,256]{0,1:T(8,128)(4,1)S(1)} %copy.38), kind=kLoop, calls=%fused_computation.23 | loop fusion | flops 1572864 | bytes 3147776 | tf_op jit(solution)/shard_map/jit(_where)/select_n | solution.py:46
  25.6 7.6 %all-to-all-start.1 = ((bf16[4,256,768]{2,0,1:T(4,128)(2,1)}), bf16[4,256,768]{2,0,1:T(4,128)(2,1)S(1)}, u32[]{:S(2)}, u32[]{:S(2)}) async-start(bf16[4,256,768]{2,0,1:T(4,128)(2,1)} %fusion.6), calls=%async_computation.1 | async-start | bytes 3145728 | tf_op jit(solution)/shard_map/all_to_all | solution.py:95
  33.4 0.2 copy.36
  33.6 6.0 %gather_fusion.1 = bf16[1024,2048]{1,0:T(8,128)(2,1)} fusion(bf16[64,2048]{1,0:T(8,128)(2,1)S(1)} %copy-done.2, s32[1024]{0:T(1024)S(1)} %broadcast_clamp_fusion), kind=kCustom, calls=%fused_computation.1 | custom fusion | bytes 8392704 | tf_op jit(solution)/shard_map/jit(_take)/gather | solution.py:50
  39.5 7.7 %multiply_convert_fusion = bf16[4,256,2048]{2,0,1:T(4,128)(2,1)} fusion(bf16[4,256,2048]{2,1,0:T(8,128)(2,1)} %bitcast.46, f32[4,256]{0,1:T(8,128)S(1)} %copy.35, pred[4,256]{0,1:T(8,128)(4,1)S(1)} %copy.36), kind=kLoop, calls=%fused_computation.9 | loop fusion | flops 8388608 | bytes 8393728 | tf_op jit(solution)/shard_map/convert_element_type | solution.py:51
  47.3 6.5 %all-to-all-done.1 = bf16[4,256,768]{2,0,1:T(4,128)(2,1)S(1)} async-done(((bf16[4,256,768]{2,0,1:T(4,128)(2,1)}), bf16[4,256,768]{2,0,1:T(4,128)(2,1)S(1)}, u32[]{:S(2)}, u32[]{:S(2)}) %all-to-all-start.1) | async-done | bytes 1572896 | tf_op jit(solution)/shard_map/all_to_all | solution.py:95
  53.8 5.4 %all-to-all-start = ((bf16[4,256,2048]{2,0,1:T(4,128)(2,1)}), bf16[4,256,2048]{2,0,1:T(4,128)(2,1)}, u32[]{:S(2)}, u32[]{:S(2)}) async-start(bf16[4,256,2048]{2,0,1:T(4,128)(2,1)} %multiply_convert_fusion), calls=%async_computation | async-start | bytes 8388608 | tf_op jit(solution)/shard_map/all_to_all | solution.py:96
  59.3 0.2 copy.42
  59.5 47.0 %all-to-all-done = bf16[4,256,2048]{2,0,1:T(4,128)(2,1)} async-done(((bf16[4,256,2048]{2,0,1:T(4,128)(2,1)}), bf16[4,256,2048]{2,0,1:T(4,128)(2,1)}, u32[]{:S(2)}, u32[]{:S(2)}) %all-to-all-start) | async-done | bytes 4194336 | tf_op jit(solution)/shard_map/all_to_all | solution.py:96
  106.5 6.4 %copy.41 = bf16[4,256,2048]{2,1,0:T(8,128)(2,1)} copy(bf16[4,256,2048]{2,0,1:T(4,128)(2,1)} %all-to-all-done) | data formatting | bytes 8388608 | tf_op jit(solution)/shard_map/while | solution.py:110
  112.9 58.6 %while.13 = (s32[]{:T(128)}, bf16[16,512,768]{2,1,0:T(8,128)(2,1)}, s32[16]{0:T(128)S(1)}, bf16[4,256,2048]{2,1,0:T(8,128)(2,1)}, bf16[4,256,768]{2,1,0:T(8,128)...) while((s32[]{:T(128)}, bf16[16,512,768]{2,1,0:T(8,128)(2,1)}, ...), condition=%wide.region_6.7_spmd, body=%wide.region_5.6_spmd.sunk | while | flops 201326624 | bytes 2228700 | solution.py:110
  112.9 0.6 dynamic_slice.48
  114.2 2.4 bitcast_dynamic-update-slice_fusion.2
  116.6 0.6 dynamic_slice.48
  117.8 2.4 bitcast_dynamic-update-slice_fusion.2
  120.2 0.6 dynamic_slice.48
  121.5 2.4 bitcast_dynamic-update-slice_fusion.2
  123.9 0.6 dynamic_slice.48
  125.2 2.4 bitcast_dynamic-update-slice_fusion.2
  127.5 0.6 dynamic_slice.48
  128.8 2.4 bitcast_dynamic-update-slice_fusion.2
  131.2 0.6 dynamic_slice.48
  132.4 2.4 bitcast_dynamic-update-slice_fusion.2
  134.8 0.6 dynamic_slice.48
  136.1 2.4 bitcast_dynamic-update-slice_fusion.2
  138.5 0.6 dynamic_slice.48
  139.7 2.4 bitcast_dynamic-update-slice_fusion.2
  142.1 0.6 dynamic_slice.48
  143.4 2.4 bitcast_dynamic-update-slice_fusion.2
  145.8 0.6 dynamic_slice.48
  147.0 2.4 bitcast_dynamic-update-slice_fusion.2
  149.4 0.6 dynamic_slice.48
  150.7 2.4 bitcast_dynamic-update-slice_fusion.2
  153.1 0.6 dynamic_slice.48
  154.4 2.4 bitcast_dynamic-update-slice_fusion.2
  156.9 0.6 dynamic_slice.48
  158.1 2.4 bitcast_dynamic-update-slice_fusion.2
  160.5 0.6 dynamic_slice.48
  161.8 2.4 bitcast_dynamic-update-slice_fusion.2
  164.2 0.6 dynamic_slice.48
  165.4 2.4 bitcast_dynamic-update-slice_fusion.2
  167.8 0.6 dynamic_slice.48
  169.1 2.4 bitcast_dynamic-update-slice_fusion.2
  171.5 86.8 %reduce-scatter.2.cloned.1.call-done = bf16[512,768]{1,0:T(8,128)(2,1)} async-done(((bf16[8192,768]{1,0:T(8,128)(2,1)}), bf16[512,768]{1,0:T(8,128)(2,1)}) %reduce-scatter.2.cloned.1.call-update) | async-done | bytes 786448 | tf_op jit(solution)/shard_map/reduce_scatter | solution.py:113
  258.3 2.8 fusion.20
  261.1 1.9 collective-permute-start
  263.1 2.1 collective-permute-done
  265.3 2.1 fusion.19
  267.4 35.7 %collective-permute-done.1 = bf16[1024,768]{1,0:T(8,128)(2,1)} collective-permute-done((bf16[1024,768]{1,0:T(8,128)(2,1)S(1)}, bf16[1024,768]{1,0:T(8,128)(2,1)}, u32[]{:S(2)}, u32[]{:S(2)}) %collective-permute-start.1) | collective-permute-done | bytes 1572896 | tf_op jit(solution)/shard_map/ppermute | solution.py:23
  303.1 1.6 convert_element_type.82
  304.8 2.2 multiply_reduce_fusion
  307.7 3.7 %divide_convert_fusion = bf16[2048,768]{1,0:T(8,128)(2,1)S(1)} fusion(f32[1024,768]{1,0:T(8,128)} %get-tuple-element.121, f32[1024,768]{1,0:T(8,128)S(1)} %convert_element_type.82, f32[]{:T(128)S(6)} %add.168, pred[]{:T(512)S(6)} %eq.50), kind=kLoop, calls=%fused_computation.12 | loop fusion | flops 7864320 | bytes 9437189 | tf_op jit(solution)/shard_map/convert_element_type | solution.py:131
  311.4 1.6 copy-done.4
  313.1 3.8 %convolution_convert_fusion.1 = bf16[768,768]{1,0:T(8,128)(2,1)} fusion(bf16[2048,768]{1,0:T(8,128)(2,1)S(1)} %divide_convert_fusion), kind=kOutput, calls=%fused_computation.26 | convolution fusion | flops 2416508928 | bytes 4325376 | tf_op jit(solution)/shard_map/dot_general | solution.py:63
  316.8 7.5 %add_convert_fusion = bf16[2048,768]{1,0:T(8,128)(2,1)S(1)} fusion(bf16[2048,768]{1,0:T(8,128)(2,1)} %copy-done.4, bf16[768,768]{1,0:T(8,128)(2,1)} %convolution_convert_fusion.1), kind=kOutput, calls=%fused_computation.11 | convolution fusion | flops 3331129344 | bytes 7471104 | tf_op jit(solution)/shard_map/dot_general | solution.py:58
  324.3 1.7 copy-done.6
  326.0 3.7 %convolution_convert_fusion = bf16[768,768]{1,0:T(8,128)(2,1)} fusion(bf16[2048,768]{1,0:T(8,128)(2,1)S(1)} %add_convert_fusion), kind=kOutput, calls=%fused_computation.25 | convolution fusion | flops 2416508928 | bytes 4325376 | tf_op jit(solution)/shard_map/dot_general | solution.py:63
  329.7 9.2 %fusion.7 = f32[2048,768]{1,0:T(8,128)} fusion(bf16[2048,768]{1,0:T(8,128)(2,1)} %copy-done.6, bf16[768,768]{1,0:T(8,128)(2,1)} %convolution_convert_fusion), kind=kOutput, calls=%fused_computation.27 | convolution fusion | flops 3324837888 | bytes 10616832 | tf_op jit(solution)/shard_map/dot_general | solution.py:58
  338.9 2.7 multiply_convert_fusion.1
  (44 shorter events, 1.7 us)
Async XLA Ops:
  7.2 9.8 %copy-start = (bf16[64,8,768]{2,1,0:T(8,128)(2,1)S(1)}, bf16[64,8,768]{2,1,0:T(8,128)(2,1)}, u32[]{:S(2)}) copy-start(bf16[64,8,768]{2,1,0:T(8,128)(2,1)} %param.7) | copy-start | bytes 2359300
  21.3 12.2 %copy-start.2 = (bf16[64,2048]{1,0:T(8,128)(2,1)S(1)}, bf16[64,2048]{1,0:T(8,128)(2,1)}, u32[]{:S(2)}) copy-start(bf16[64,2048]{1,0:T(8,128)(2,1)} %param.8) | copy-start | bytes 786436
  25.6 28.2 %all-to-all-start.1 = ((bf16[4,256,768]{2,0,1:T(4,128)(2,1)}), bf16[4,256,768]{2,0,1:T(4,128)(2,1)S(1)}, u32[]{:S(2)}, u32[]{:S(2)}) async-start(bf16[4,256,768]{2,0,1:T(4,128)(2,1)} %fusion.6), calls=%async_computation.1 | async-start | bytes 3145728 | tf_op jit(solution)/shard_map/all_to_all | solution.py:95
  53.8 52.7 %all-to-all-start = ((bf16[4,256,2048]{2,0,1:T(4,128)(2,1)}), bf16[4,256,2048]{2,0,1:T(4,128)(2,1)}, u32[]{:S(2)}, u32[]{:S(2)}) async-start(bf16[4,256,2048]{2,0,1:T(4,128)(2,1)} %multiply_convert_fusion), calls=%async_computation | async-start | bytes 8388608 | tf_op jit(solution)/shard_map/all_to_all | solution.py:96
  59.2 199.1 %reduce-scatter.2.cloned.1.call-start = ((), (), s32[]{:S(2)}) async-start(), calls=%async_computation.3 | async-start | bytes 13369344 | tf_op jit(solution)/shard_map/reduce_scatter | solution.py:113
  171.5 86.8 %copy-start.5 = (f32[512,768]{1,0:T(8,128)S(1)}, f32[512,768]{1,0:T(8,128)}, u32[]{:S(2)}) copy-start(f32[512,768]{1,0:T(8,128)} %param.11) | copy-start | bytes 4718596
  261.1 4.0 %collective-permute-start = (bf16[512,768]{1,0:T(8,128)(2,1)}, bf16[512,768]{1,0:T(8,128)(2,1)S(1)}, u32[]{:S(2)}, u32[]{:S(2)}) collective-permute-start(bf16[512,768]{1,0:T(8,128)(2,1)} %get-tuple-element.122), channel_id=1, source_target_pairs={{0,16},{16,0},{32,48},{48,32},{64,80},{80,64},{96,112},{112,96},{1... | collective-permute-start | bytes 2359304 | tf_op jit(solution)/shard_map/ppermute | solution.py:23
  267.4 35.7 %collective-permute-start.1 = (bf16[1024,768]{1,0:T(8,128)(2,1)S(1)}, bf16[1024,768]{1,0:T(8,128)(2,1)}, u32[]{:S(2)}, u32[]{:S(2)}) collective-permute-start(bf16[1024,768]{1,0:T(8,128)(2,1)S(1)} %get-tuple-element.120), channel_id=1, source_target_pairs={{0,32},{32,0},{16,48},{48,16},{64,96},{96,64},{80,112},{112,80},{1... | collective-permute-start | bytes 4718600 | tf_op jit(solution)/shard_map/ppermute | solution.py:23
  267.4 37.4 %copy-start.3 = (f32[1024,768]{1,0:T(8,128)S(1)}, f32[1024,768]{1,0:T(8,128)}, u32[]{:S(2)}) copy-start(f32[1024,768]{1,0:T(8,128)} %get-tuple-element.121) | copy-start | bytes 9437188
  311.4 1.7 copy-start.4
  324.3 1.7 copy-start.6
  329.7 11.9 %copy-start.1 = (bf16[64,8,768]{2,1,0:T(8,128)(2,1)S(1)}, bf16[64,8,768]{2,1,0:T(8,128)(2,1)}, u32[]{:S(2)}) copy-start(bf16[64,8,768]{2,1,0:T(8,128)(2,1)} %param.7) | copy-start | bytes 2359300
Sparse Core Ops, SparseCore 0:
  171.6 86.6 reduce-scatter.1
where the time goes:
time: 350 us; the launch traced here: 348 us
  waiting for transfers between devices  178 us (51%)
  matrix products  62.3 us (18%)
  local copies, waits for them, and re-layouts  39 us (11%)
  other arithmetic  28 us (8%)
  between operations  15 us (4%)
  starting transfers between devices  14.9 us (4%)
  loops' own time  11.1 us (3%)
    reduce_scatter x1, waiting for transfers between devices, body(): lax.psum_scatter(blocks.reshape(own_rows * lax.axis_size('dp'), hidden_wi...  86.8 us
    all_to_all x1, waiting for transfers between devices, body(): lax.all_to_all(weighted_send, 'expert', split_axis=1, concat_axis=1, tile...  47 us
    dot_general x16, matrix products, block_rows(): lax.dot_general(columns, hidden_expert, (((0,), (0,)), ((), ())), preferr...  38.2 us
    ppermute x2, waiting for transfers between devices, swapped(): return lax.ppermute(block, axis, route)  37.8 us
    dot_general x2, matrix products, newton_update(): product = jnp.dot(scaled, poly, preferred_element_type=jnp.float32)  16.7 us
    another operation x1, loops' own time, body(): lax.map(block_rows, jnp.arange(own_rows * lax.axis_size('dp') // own_rows...  11.1 us
    dynamic_slice x16, local copies, waits for them, and re-layouts, body(): lax.map(block_rows, jnp.arange(own_rows * lax.axis_size('dp') // own_rows...  9.32 us
    convert_element_type x1, other arithmetic, pack_slots(): weighted = (scales[..., None] * grad_rows).astype(jnp.bfloat16)  7.74 us
  transfers between devices with their start and end apart: 5, of which 5 were waited for; matrix products, arithmetic and copies ran while one was open for 4% of the time, Pallas kernels for 0%

commit v1 on v0

--- a/solution.py
+++ b/solution.py
@@ -11,6 +11,12 @@
 COEFF_B = -4.775
 COEFF_C = 2.0315
 EPSILON = 1e-07
+
+
+def trade_parts(x, name, split, join):
+    parts = jnp.split(x, lax.axis_size(name), axis=split)
+    received = lax.all_to_all(jnp.stack(parts), name, 0, 0)
+    return jnp.concatenate(received, axis=join)
 
 
 def swapped(block, axis, apart):
@@ -92,7 +98,7 @@
         activations, out_grad, gate_weights, source, filled, slots_token
     )
     hidden_got, weighted_got = (
-        lax.all_to_all(hidden_send, "expert", split_axis=1, concat_axis=1, tiled=True),
+        trade_parts(hidden_send, "expert", 1, 1),
         lax.all_to_all(weighted_send, "expert", split_axis=1, concat_axis=1, tiled=True),
     )
 

time: 350 us -> 356 us (1.017)
  local copies, waits for them, and re-layouts: 39 us -> 48.9 us
  other arithmetic: 28 us -> 24.2 us
    unnamed x18 -> x33, local copies, waits for them, and re-layouts: 4.99 us -> 14.7 us
    select_n x1, other arithmetic: 4.26 us -> 0.45 us  [pack_slots(): jnp.where(filled[..., None], jnp.take(hidden_rows, source, axis=0), jnp.z...]
where the time goes in v1:
time: 356 us; the launch traced here: 355 us
  waiting for transfers between devices  178 us (50%)
  matrix products  62.3 us (18%)
  local copies, waits for them, and re-layouts  48.9 us (14%)
  other arithmetic  24.2 us (7%)
  starting transfers between devices  15.1 us (4%)
  between operations  15 us (4%)
  loops' own time  11.1 us (3%)
    reduce_scatter x1, waiting for transfers between devices, body(): lax.psum_scatter(blocks.reshape(own_rows * lax.axis_size('dp'), hidden_wi...  86.8 us
    all_to_all x1, waiting for transfers between devices, body(): lax.all_to_all(weighted_send, 'expert', split_axis=1, concat_axis=1, tile...  47.1 us
    dot_general x16, matrix products, block_rows(): lax.dot_general(columns, hidden_expert, (((0,), (0,)), ((), ())), preferr...  38.1 us
    ppermute x2, waiting for transfers between devices, swapped(): return lax.ppermute(block, axis, route)  37.8 us
    dot_general x2, matrix products, newton_update(): product = jnp.dot(scaled, poly, preferred_element_type=jnp.float32)  16.7 us
    unnamed x33, local copies, waits for them, and re-layouts  14.7 us
    another operation x1, loops' own time, body(): lax.map(block_rows, jnp.arange(own_rows * lax.axis_size('dp') // own_rows...  11.1 us
    dynamic_slice x16, local copies, waits for them, and re-layouts, body(): lax.map(block_rows, jnp.arange(own_rows * lax.axis_size('dp') // own_rows...  9.32 us
  transfers between devices with their start and end apart: 5, of which 5 were waited for; matrix products, arithmetic and copies ran while one was open for 4% of the time, Pallas kernels for 0%

profile of v1, /device:TPU:1, one launch (start us, length us, event | category | flops | bytes accessed | tf_op | source)
XLA Modules:
  0.0 354.7 jit_solution(17353037474297925907)
XLA Ops:
  7.2 0.8 copy.28
  8.9 0.8 copy.33
  9.8 6.9 %gather_fusion = f32[1024]{0:T(1024)S(1)} fusion(f32[512]{0:T(512)S(1)} %reshape.208, s32[1024]{0:T(1024)S(1)} %get-tuple-element.130), kind=kCustom, calls=%fused_computation | custom fusion | bytes 12288 | tf_op jit(solution)/shard_map/jit(_take)/gather | solution.py:55
  16.9 4.0 %gather_fusion.2 = bf16[1024,768]{1,0:T(8,128)(2,1)S(1)} fusion(bf16[512,768]{1,0:T(8,128)(2,1)S(1)} %bitcast.111, s32[1024]{0:T(1024)S(1)} %get-tuple-element.130), kind=kCustom, calls=%fused_computation.2 | custom fusion | bytes 3149824 | tf_op jit(solution)/shard_map/jit(_take)/gather | solution.py:53
  21.4 0.6 fusion.23
  22.1 0.6 fusion.22
  22.7 0.6 fusion.21
  23.4 0.6 fusion.20
  24.0 0.6 fusion.19
  24.7 0.6 fusion.18
  25.3 0.6 fusion.17
  26.0 0.6 fusion.16
  26.6 0.6 fusion.15
  27.3 0.6 fusion.14
  27.9 0.6 fusion.13
  28.5 0.6 fusion.12
  29.2 0.6 fusion.11
  29.8 0.6 fusion.10
  30.5 0.6 fusion.9
  31.1 0.6 fusion.8
  31.8 7.7 %all-to-all-start.1 = ((bf16[16,4,16,768]{3,2,1,0:T(8,128)(2,1)}), bf16[16,4,16,768]{3,2,1,0:T(8,128)(2,1)S(1)}, u32[]{:S(2)}, u32[]{:S(2)}) async-start(bf16[16,4,16,768]{3,2,1,0:T(8,128)(2,1)} %fusion.8), calls=%async_computation.1 | async-start | bytes 3145728 | tf_op jit(solution)/shard_map/all_to_all | solution.py:18
  39.9 6.0 %gather_fusion.1 = bf16[1024,2048]{1,0:T(8,128)(2,1)} fusion(bf16[64,2048]{1,0:T(8,128)(2,1)S(1)} %copy-done.2, s32[1024]{0:T(1024)S(1)} %get-tuple-element.129), kind=kCustom, calls=%fused_computation.1 | custom fusion | bytes 8392704 | tf_op jit(solution)/shard_map/jit(_take)/gather | solution.py:56
  45.9 7.7 %multiply_convert_fusion = bf16[4,256,2048]{2,0,1:T(4,128)(2,1)} fusion(bf16[4,256,2048]{2,1,0:T(8,128)(2,1)} %bitcast.112, f32[4,256]{0,1:T(8,128)S(1)} %copy.35, pred[4,256]{0,1:T(8,128)(4,1)S(1)} %copy.36), kind=kLoop, calls=%fused_computation.9 | loop fusion | flops 8388608 | bytes 8393728 | tf_op jit(solution)/shard_map/convert_element_type | solution.py:57
  53.6 6.5 %all-to-all-done.1 = bf16[16,4,16,768]{3,2,1,0:T(8,128)(2,1)S(1)} async-done(((bf16[16,4,16,768]{3,2,1,0:T(8,128)(2,1)}), bf16[16,4,16,768]{3,2,1,0:T(8,128)(2,1)S(1)}, u32[]{:S(2)}, u32[]{:S(2)}) %all-to-all-start.1) | async-done | bytes 1572896 | tf_op jit(solution)/shard_map/all_to_all | solution.py:18
  60.1 5.4 %all-to-all-start = ((bf16[4,256,2048]{2,0,1:T(4,128)(2,1)}), bf16[4,256,2048]{2,0,1:T(4,128)(2,1)}, u32[]{:S(2)}, u32[]{:S(2)}) async-start(bf16[4,256,2048]{2,0,1:T(4,128)(2,1)} %multiply_convert_fusion), calls=%async_computation | async-start | bytes 8388608 | tf_op jit(solution)/shard_map/all_to_all | solution.py:102
  65.7 47.1 %all-to-all-done = bf16[4,256,2048]{2,0,1:T(4,128)(2,1)} async-done(((bf16[4,256,2048]{2,0,1:T(4,128)(2,1)}), bf16[4,256,2048]{2,0,1:T(4,128)(2,1)}, u32[]{:S(2)}, u32[]{:S(2)}) %all-to-all-start) | async-done | bytes 4194336 | tf_op jit(solution)/shard_map/all_to_all | solution.py:102
  112.8 6.4 %copy.39 = bf16[4,256,2048]{2,1,0:T(8,128)(2,1)} copy(bf16[4,256,2048]{2,0,1:T(4,128)(2,1)} %all-to-all-done) | data formatting | bytes 8388608 | tf_op jit(solution)/shard_map/while | solution.py:116
  119.2 58.5 %while.13 = (s32[]{:T(128)}, bf16[16,512,768]{2,1,0:T(8,128)(2,1)}, s32[16]{0:T(128)S(1)}, bf16[4,256,2048]{2,1,0:T(8,128)(2,1)}, bf16[4,256,768]{2,1,0:T(8,128)...) while((s32[]{:T(128)}, bf16[16,512,768]{2,1,0:T(8,128)(2,1)}, ...), condition=%wide.region_6.7_spmd, body=%wide.region_5.6_spmd.sunk | while | flops 201326624 | bytes 2229200 | solution.py:116
  119.2 0.6 dynamic_slice.48
  120.5 2.4 bitcast_dynamic-update-slice_fusion.2
  124.1 2.4 bitcast_dynamic-update-slice_fusion.2
  127.8 2.4 bitcast_dynamic-update-slice_fusion.2
  130.2 0.6 dynamic_slice.48
  131.5 2.4 bitcast_dynamic-update-slice_fusion.2
  133.8 0.6 dynamic_slice.48
  135.1 2.4 bitcast_dynamic-update-slice_fusion.2
  138.7 2.4 bitcast_dynamic-update-slice_fusion.2
  142.4 2.4 bitcast_dynamic-update-slice_fusion.2
  146.1 2.4 bitcast_dynamic-update-slice_fusion.2
  149.7 2.4 bitcast_dynamic-update-slice_fusion.2
  152.1 0.6 dynamic_slice.48
  153.3 2.4 bitcast_dynamic-update-slice_fusion.2
  157.0 2.5 bitcast_dynamic-update-slice_fusion.2
  160.7 2.4 bitcast_dynamic-update-slice_fusion.2
  164.4 2.4 bitcast_dynamic-update-slice_fusion.2
  168.1 2.4 bitcast_dynamic-update-slice_fusion.2
  171.7 2.4 bitcast_dynamic-update-slice_fusion.2
  175.4 2.4 bitcast_dynamic-update-slice_fusion.2
  177.8 86.8 %reduce-scatter.2.cloned.1.call-done = bf16[512,768]{1,0:T(8,128)(2,1)} async-done(((bf16[8192,768]{1,0:T(8,128)(2,1)}), bf16[512,768]{1,0:T(8,128)(2,1)}) %reduce-scatter.2.cloned.1.call-update) | async-done | bytes 786448 | tf_op jit(solution)/shard_map/reduce_scatter | solution.py:119
  264.6 2.8 fusion.35
  267.4 1.9 collective-permute-start
  269.3 2.1 collective-permute-done
  271.6 2.1 fusion.34
  273.7 35.7 %collective-permute-done.1 = bf16[1024,768]{1,0:T(8,128)(2,1)} collective-permute-done((bf16[1024,768]{1,0:T(8,128)(2,1)S(1)}, bf16[1024,768]{1,0:T(8,128)(2,1)}, u32[]{:S(2)}, u32[]{:S(2)}) %collective-permute-start.1) | collective-permute-done | bytes 1572896 | tf_op jit(solution)/shard_map/ppermute | solution.py:29
  309.4 1.6 convert_element_type.82
  311.1 2.2 multiply_reduce_fusion
  314.0 3.6 %divide_convert_fusion = bf16[2048,768]{1,0:T(8,128)(2,1)S(1)} fusion(f32[1024,768]{1,0:T(8,128)} %get-tuple-element.121, f32[1024,768]{1,0:T(8,128)S(1)} %convert_element_type.82, f32[]{:T(128)S(6)} %add.168, pred[]{:T(512)S(6)} %eq.50), kind=kLoop, calls=%fused_computation.12 | loop fusion | flops 7864320 | bytes 9437189 | tf_op jit(solution)/shard_map/convert_element_type | solution.py:137
  317.7 1.6 copy-done.4
  319.3 3.8 %convolution_convert_fusion.1 = bf16[768,768]{1,0:T(8,128)(2,1)} fusion(bf16[2048,768]{1,0:T(8,128)(2,1)S(1)} %divide_convert_fusion), kind=kOutput, calls=%fused_computation.25 | convolution fusion | flops 2416508928 | bytes 4325376 | tf_op jit(solution)/shard_map/dot_general | solution.py:69
  323.1 7.5 %add_convert_fusion = bf16[2048,768]{1,0:T(8,128)(2,1)S(1)} fusion(bf16[2048,768]{1,0:T(8,128)(2,1)} %copy-done.4, bf16[768,768]{1,0:T(8,128)(2,1)} %convolution_convert_fusion.1), kind=kOutput, calls=%fused_computation.11 | convolution fusion | flops 3331129344 | bytes 7471104 | tf_op jit(solution)/shard_map/dot_general | solution.py:64
  330.6 1.7 copy-done.6
  332.3 3.7 %convolution_convert_fusion = bf16[768,768]{1,0:T(8,128)(2,1)} fusion(bf16[2048,768]{1,0:T(8,128)(2,1)S(1)} %add_convert_fusion), kind=kOutput, calls=%fused_computation.24 | convolution fusion | flops 2416508928 | bytes 4325376 | tf_op jit(solution)/shard_map/dot_general | solution.py:69
  335.9 9.2 %fusion.6 = f32[2048,768]{1,0:T(8,128)} fusion(bf16[2048,768]{1,0:T(8,128)(2,1)} %copy-done.6, bf16[768,768]{1,0:T(8,128)(2,1)} %convolution_convert_fusion), kind=kOutput, calls=%fused_computation.26 | convolution fusion | flops 3324837888 | bytes 10616832 | tf_op jit(solution)/shard_map/dot_general | solution.py:64
  345.1 2.7 multiply_convert_fusion.1
  (57 shorter events, 9.3 us)
Async XLA Ops:
  7.2 9.8 %copy-start = (bf16[64,8,768]{2,1,0:T(8,128)(2,1)S(1)}, bf16[64,8,768]{2,1,0:T(8,128)(2,1)}, u32[]{:S(2)}) copy-start(bf16[64,8,768]{2,1,0:T(8,128)(2,1)} %param.7) | copy-start | bytes 2359300
  31.8 8.1 %copy-start.2 = (bf16[64,2048]{1,0:T(8,128)(2,1)S(1)}, bf16[64,2048]{1,0:T(8,128)(2,1)}, u32[]{:S(2)}) copy-start(bf16[64,2048]{1,0:T(8,128)(2,1)} %param.8) | copy-start | bytes 786436
  31.8 28.3 %all-to-all-start.1 = ((bf16[16,4,16,768]{3,2,1,0:T(8,128)(2,1)}), bf16[16,4,16,768]{3,2,1,0:T(8,128)(2,1)S(1)}, u32[]{:S(2)}, u32[]{:S(2)}) async-start(bf16[16,4,16,768]{3,2,1,0:T(8,128)(2,1)} %fusion.8), calls=%async_computation.1 | async-start | bytes 3145728 | tf_op jit(solution)/shard_map/all_to_all | solution.py:18
  60.1 52.7 %all-to-all-start = ((bf16[4,256,2048]{2,0,1:T(4,128)(2,1)}), bf16[4,256,2048]{2,0,1:T(4,128)(2,1)}, u32[]{:S(2)}, u32[]{:S(2)}) async-start(bf16[4,256,2048]{2,0,1:T(4,128)(2,1)} %multiply_convert_fusion), calls=%async_computation | async-start | bytes 8388608 | tf_op jit(solution)/shard_map/all_to_all | solution.py:102
  65.5 199.0 %reduce-scatter.2.cloned.1.call-start = ((), (), s32[]{:S(2)}) async-start(), calls=%async_computation.3 | async-start | bytes 13369344 | tf_op jit(solution)/shard_map/reduce_scatter | solution.py:119
  177.7 86.8 %copy-start.5 = (f32[512,768]{1,0:T(8,128)S(1)}, f32[512,768]{1,0:T(8,128)}, u32[]{:S(2)}) copy-start(f32[512,768]{1,0:T(8,128)} %param.11) | copy-start | bytes 4718596
  267.4 4.0 %collective-permute-start = (bf16[512,768]{1,0:T(8,128)(2,1)}, bf16[512,768]{1,0:T(8,128)(2,1)S(1)}, u32[]{:S(2)}, u32[]{:S(2)}) collective-permute-start(bf16[512,768]{1,0:T(8,128)(2,1)} %get-tuple-element.122), channel_id=1, source_target_pairs={{0,16},{16,0},{32,48},{48,32},{64,80},{80,64},{96,112},{112,96},{1... | collective-permute-start | bytes 2359304 | tf_op jit(solution)/shard_map/ppermute | solution.py:29
  273.7 35.7 %collective-permute-start.1 = (bf16[1024,768]{1,0:T(8,128)(2,1)S(1)}, bf16[1024,768]{1,0:T(8,128)(2,1)}, u32[]{:S(2)}, u32[]{:S(2)}) collective-permute-start(bf16[1024,768]{1,0:T(8,128)(2,1)S(1)} %get-tuple-element.120), channel_id=1, source_target_pairs={{0,32},{32,0},{16,48},{48,16},{64,96},{96,64},{80,112},{112,80},{1... | collective-permute-start | bytes 4718600 | tf_op jit(solution)/shard_map/ppermute | solution.py:29
  273.7 37.4 %copy-start.3 = (f32[1024,768]{1,0:T(8,128)S(1)}, f32[1024,768]{1,0:T(8,128)}, u32[]{:S(2)}) copy-start(f32[1024,768]{1,0:T(8,128)} %get-tuple-element.121) | copy-start | bytes 9437188
  317.7 1.6 copy-start.4
  330.6 1.7 copy-start.6
  335.9 11.9 %copy-start.1 = (bf16[64,8,768]{2,1,0:T(8,128)(2,1)S(1)}, bf16[64,8,768]{2,1,0:T(8,128)(2,1)}, u32[]{:S(2)}) copy-start(bf16[64,8,768]{2,1,0:T(8,128)(2,1)} %param.7) | copy-start | bytes 2359300
Sparse Core Ops, SparseCore 0:
  177.9 86.6 reduce-scatter.1
